TPU v7x, 256 devices: a whole 4x4x8 slice. The times are simulated.
256 devices in a mesh: grid: 64 (over y, x, z_lo, core), rep: 4 (over z_hi).
Axes of the slice: x: 4, y: 4, z: 8 (z_hi: 4, z_lo: 2; z = z_hi * 2 + z_lo), core: 2. Of those that a mesh axis runs over, the one named last changes fastest.
Arguments:
- amplitudes: bfloat16 [2, 832, 13312], P(None, 'grid', 'rep'), may hold values from -6 to 6
- integrals: bfloat16 [8, 13312, 13312], P(None, 'grid', 'rep'), may hold values from -0.0546875 to 0.0546875
- virt_size: int32 [8], replicated, may hold values from 60 to 208, as said below
- slab: int32 [2], replicated, may hold values from 0 to 127
Outputs:
- residual: float32 [2, 832, 13312], P(None, 'grid', 'rep')
Inputs may be any that keep to these rules, and one draw needn't show every extreme that they name: `virt_size`: the sizes sum to 832; exactly one symmetry block holds 208 virtual orbitals, all others fewer.
All inputs are finite; a program needn't handle non-finite values.
Results may differ from a plain program's by a relative error of at most 0.0003.
Values may be sent and summed in bfloat16 or wider, within the bound.
A program may use at most 256 MiB of HBM per device.

v0:
```python
import jax
import jax.numpy as jnp
from jax import lax
from jax.sharding import PartitionSpec as P

NIRREP = 8
O = 128


def accumulate(whole, integrals, virt_size, occ_irrep):
    member_count, virt_count, _ = whole.shape
    window = virt_count // 4
    offsets = jnp.cumsum(virt_size) - virt_size
    anchors = jnp.minimum(offsets, virt_count - window)
    labels = lax.broadcasted_iota(jnp.int32, (1, NIRREP), 1)
    rows = lax.broadcasted_iota(jnp.int32, (virt_count, 1), 0)
    row_irrep = jnp.sum((rows >= offsets[None, :]).astype(jnp.int32), axis=1) - 1
    onehot = (row_irrep[:, None] == labels).astype(jnp.int32)
    row_anchor = jnp.sum(onehot * anchors[None, :], axis=1)
    pick = row_irrep * window + rows[:, 0] - row_anchor
    results = []
    for member in range(member_count):
        blocks = []
        for irrep_a in range(NIRREP):
            pair_irrep = jnp.bitwise_xor(occ_irrep[member], irrep_a)
            block_w = lax.dynamic_index_in_dim(integrals, pair_irrep, 0, keepdims=False)
            window_rows = lax.dynamic_slice_in_dim(whole[member], anchors[irrep_a], window, 0)
            blocks.append(
                lax.dot_general(
                    window_rows,
                    block_w,
                    (((1,), (1,)), ((), ())),
                    preferred_element_type=jnp.float32,
                )
            )
        stacked = jnp.concatenate(blocks, axis=0)
        results.append(jnp.take(stacked, pick, axis=0))
    return jnp.stack(results, axis=0)


def per_device(amplitudes, integrals, virt_size, slab):
    whole = lax.all_gather(amplitudes, "grid", axis=1, tiled=True)
    occ_irrep = slab // (O // NIRREP)
    partial_value = accumulate(whole, integrals, virt_size, occ_irrep)
    exchanged = lax.all_to_all(partial_value, "grid", split_axis=1, concat_axis=2, tiled=True)
    return lax.psum_scatter(exchanged, "rep", scatter_dimension=2, tiled=True)


def solution(mesh):
    return jax.shard_map(
        per_device,
        mesh=mesh,
        in_specs=(P(None, "grid", "rep"), P(None, "grid", "rep"), P(), P()),
        out_specs=P(None, "grid", "rep"),
        check_vma=False,
    )
```

profile of v0, /device:TPU:16, one launch (start us, length us, event | category | flops | bytes accessed | tf_op | source)
XLA Modules:
  0.0 571.5 jit_solution(10626723796836507561)
XLA Ops:
  20.4 0.8 reduce-window.9
  39.8 90.1 %all-gather.2.cloned.1.call-done = bf16[2,832,3328]{2,0,1:T(2,128)(2,1)} async-done(((bf16[2,13,3328]{2,0,1:T(2,128)(2,1)}), bf16[2,832,3328]{2,0,1:T(2,128)(2,1)}) %all-gather.2.cloned.1.call-update) | async-done | bytes 11075600 | tf_op jit(solution)/shard_map/all_gather | solution.py:42
  129.8 22.4 %fusion.64 = (bf16[1,832,3328]{2,0,1:T(2,128)(2,1)S(1)}, bf16[1,832,3328]{2,0,1:T(2,128)(2,1)}) fusion(bf16[2,832,3328]{2,0,1:T(2,128)(2,1)} %all-gather.2.cloned.1.call-done), kind=kLoop, calls=%fused_computation.115 | loop fusion | bytes 22151168 | tf_op jit(solution)/shard_map/slice | solution.py:27
  152.2 50.9 %constant_dynamic-slice_fusion = (bf16[1,208,3328]{2,0,1:T(2,128)(2,1)}, bf16[1,208,3328]{2,0,1:T(2,128)(2,1)}, bf16[1,208,3328]{2,0,1:T(2,128)(2,1)}, bf16[1,20...) fusion(bf16[1,832,3328]{2,0,1:T(2,128)(2,1)} %get-tuple-element, ...), kind=kLoop, calls=%fused_computation.75 | loop fusion | bytes 44302368 | tf_op jit(solution)/shard_map/dynamic_slice | solution.py:27
  203.1 2.9 fusion.15
  206.2 2.0 fusion.14
  208.2 2.7 fusion.13
  211.0 2.6 fusion.12
  213.6 2.6 fusion.11
  216.1 2.6 fusion.10
  218.7 2.0 fusion.9
  220.7 1.9 fusion.8
  222.6 1.0 concatenate.6
  224.2 2.9 fusion
  227.2 2.0 fusion.1
  229.3 2.1 fusion.2
  231.3 2.1 fusion.3
  233.4 2.1 fusion.4
  235.5 2.1 fusion.5
  237.6 1.9 fusion.6
  239.5 1.9 fusion.7
  241.4 1.5 concatenate.7
  242.9 1.8 copy.26
  244.8 3.4 gather_fusion
  248.2 2.7 gather_fusion.1
  251.2 1.3 copy.27
  252.5 30.0 %all_to_all.18 = f32[2,832,208]{2,0,1:T(2,128)S(1)} all-to-all(f32[2,832,208]{2,0,1:T(2,128)S(1)} %copy.27), channel_id=1, replica_groups=mesh['grid'=64,'rep'=4] {'grid'}, dimensions={1} | all-to-all | bytes 2768896 | tf_op jit(solution)/shard_map/all_to_all | solution.py:45
  282.5 52.9 %copy.31 = f32[2,13,64,208]{0,1,3,2:T(8,128)} copy(f32[2,13,64,208]{3,0,1,2:T(2,128)S(1)} %bitcast.123) | data formatting | bytes 2768896
  335.3 69.6 %reshape.76 = f32[13312,26]{1,0:T(8,128)} reshape(f32[13312,13,2]{2,1,0:T(8,128)} %bitcast.49) | data formatting | bytes 2768896
  405.0 126.1 %reduce-scatter.4.cloned.1.call-done = f32[3328,26]{1,0:T(8,128)} async-done(((f32[13312,26]{1,0:T(8,128)}), f32[3328,26]{1,0:T(8,128)}) %reduce-scatter.4.cloned.1.call-update) | async-done | bytes 346128
  531.1 16.8 %reshape.77 = f32[3328,13,2]{2,1,0:T(8,128)} reshape(f32[3328,26]{1,0:T(8,128)} %reduce-scatter.4.cloned.1.call-done) | data formatting | bytes 692224
  547.9 16.8 %copy.30 = f32[2,13,3328]{2,0,1:T(2,128)} copy(f32[2,13,3328]{0,1,2:T(8,128)} %bitcast.122) | data formatting | bytes 692224
  (48 shorter events, 4.6 us)
Async XLA Ops:
  6.5 123.3 %all-gather.2.cloned.1.call-start = ((), (), s32[]{:S(2)}) async-start(), calls=%async_computation.2 | async-start | bytes 11248640 | tf_op jit(solution)/shard_map/all_gather | solution.py:42
  7.3 523.8 %reduce-scatter.4.cloned.1.call-start = ((), (), s32[]{:S(2)}) async-start(), calls=%async_computation.3 | async-start | bytes 8519680
  203.1 3.0 copy-start.11
  203.1 5.1 copy-start.10
  206.2 4.8 copy-start.9
  208.2 5.3 copy-start.8
  218.7 3.9 copy-start.12
  218.7 3.9 copy-start.13
  218.7 3.9 copy-start.14
  218.7 3.9 copy-start.15
  224.2 3.0 copy-start.7
  224.2 5.1 copy-start.6
  227.2 4.1 copy-start.5
  229.3 4.2 copy-start.4
  231.3 4.2 copy-start.3
  233.4 4.2 copy-start.2
  235.5 4.0 copy-start.1
  248.2 2.7 copy-start
Sparse Core Ops, SparseCore 0:
  9.2 120.5 all-gather.1
  405.1 125.9 reduce-scatter.3
where the time goes:
time: 574 us; the launch traced here: 572 us
  local copies, waits for them, and re-layouts  243 us (42%)
  waiting for transfers between devices  217 us (38%)
  between operations  42.6 us (7%)
  matrix products  36.2 us (6%)
  blocking collectives  30 us (5%)
    unnamed x36, local copies, waits for them, and re-layouts  156 us
    unnamed x3, waiting for transfers between devices  127 us
    all_gather x1, waiting for transfers between devices, per_device(): whole = lax.all_gather(amplitudes, 'grid', axis=1, tiled=True)  90.1 us
    dynamic_slice x1, local copies, waits for them, and re-layouts, accumulate(): lax.dynamic_slice_in_dim(whole[member], anchors[irrep_a], window, 0)  50.9 us
    dot_general x16, matrix products, accumulate(): lax.dot_general(window_rows, block_w, (((1,), (1,)), ((), ())), preferred...  36.2 us
    all_to_all x1, blocking collectives, per_device(): lax.all_to_all(partial_value, 'grid', split_axis=1, concat_axis=2, tiled=...  30 us
    slice x1, local copies, waits for them, and re-layouts, accumulate(): whole[member]  22.4 us
  transfers between devices with their start and end apart: 2, of which 2 were waited for; matrix products, arithmetic and copies ran while one was open for 1% of the time, Pallas kernels for 0%

commit v1 on v0

v1 whole, which is shorter than its diff:
```python
import functools

import jax
import jax.numpy as jnp
from jax import lax
from jax.experimental import pallas as pl
from jax.experimental.pallas import tpu as pltpu
from jax.sharding import PartitionSpec as P

NIRREP = 8
O = 128
RING = 4
K = 3328
Q = 208
ROWS = 13
PAD = 16
QUAD = 4
PIECE = QUAD * PAD
LANES = 256
DEPTH = 256
STEPS = 32700.0
MESH = pl.DeviceIdType.MESH


def turn(o):
    return o + o // 2 - 2 * (o // 3)


def encode(value, wide):
    peak = jnp.max(jnp.abs(value), axis=1, keepdims=True)
    level = jnp.ceil(jnp.log2(jnp.maximum(peak, 1e-30)) + 0.01)
    wide[:, :Q] = jnp.round(value * (jnp.exp2(-level) * STEPS))
    wide[:, Q:] = jnp.broadcast_to(level, (value.shape[0], LANES - Q))
    return wide[...].astype(jnp.int32).astype(jnp.int16)


def decode(coded):
    value = coded.astype(jnp.int32).astype(jnp.float32)
    return value * (jnp.exp2(value[:, Q:Q + 1]) * (1.0 / STEPS))


def kernel(
    slab_ref, virt_ref, amp_ref, w_hbm, out_ref,
    buf, w_ref, wide, stage, inbox, total, final,
    w_sem, recv_sem, send_sem, pair_sem,
    part_send, part_recv, sum_send, sum_recv, step_sem, far_sem,
):
    g = lax.axis_index("grid")
    r = lax.axis_index("rep")
    c = g % 2
    zl = (g // 2) % 2
    x = (g // 4) % RING
    y = g // 16

    def grid_of(yy, xx, zz, cc):
        return ((yy * RING + xx) * 2 + zz) * 2 + cc

    def chip_of(m, a, b):
        return b + m * (a - b), a + m * (b - a)

    a0 = (x, y)
    b0 = (y, x)

    def place(m, ob, oa):
        pa = (x + m * (y - x) + turn(oa)) % RING
        pb = (y + m * (x - y) + turn(ob)) % RING
        return chip_of(m, pa, pb)

    def neighbour(m, da, db):
        na = (x + m * (y - x) + da + RING) % RING
        nb = (y + m * (x - y) + db + RING) % RING
        yy, xx = chip_of(m, na, nb)
        return grid_of(yy, xx, zl, c)

    sibling = grid_of(y, x, zl, 1 - c)
    partner = grid_of(y, x, 1 - zl, c)

    barrier = pltpu.get_barrier_semaphore()
    near = [sibling, partner] + [neighbour(0, da, db) for da, db in ((1, 0), (-1, 0), (0, 1), (0, -1))]
    for n in near:
        pl.semaphore_signal(barrier, inc=1, device_id=(n, r), device_id_type=MESH)
    beyond = (grid_of(y, x, 1 - zl, c), (r + 2 * zl + 3) % 4)
    pl.semaphore_signal(barrier, inc=1, device_id=beyond, device_id_type=MESH)

    w_copy = pltpu.make_async_copy(w_hbm, w_ref, w_sem)
    w_copy.start()
    mine = y * RING + x
    for m in range(2):
        buf[m, mine, zl * 2 + c] = jnp.zeros((PAD, K), jnp.bfloat16)
        buf[m, mine, zl * 2 + c, :ROWS, :] = amp_ref[m]

    pl.semaphore_wait(barrier, len(near) + 1)
    pl.semaphore_signal(step_sem, inc=1, device_id=(partner, r), device_id_type=MESH)
    pl.semaphore_signal(step_sem, inc=1, device_id=beyond, device_id_type=MESH)

    def block_copy(m, pos, z, cc, sem, target):
        block = buf.at[m, pos, z * 2 + cc]
        return pltpu.make_async_remote_copy(
            src_ref=block, dst_ref=block, send_sem=sem, recv_sem=recv_sem.at[m, pos, z * 2 + cc],
            device_id=(target, r), device_id_type=MESH,
        )

    def arrived(m, pos, z, cc):
        block_copy(m, pos, z, cc, pair_sem.at[0], sibling).wait_recv()

    def do(copy, starting):
        if starting:
            copy.start()
        else:
            copy.wait_send()

    def own_pair(m, starting):
        do(block_copy(m, mine, zl, c, pair_sem.at[m], partner), starting)

    def relay(m, ob, oa, phase, starting):
        yy, xx = place(m, ob, oa)
        pos = yy * RING + xx
        for z in range(2):
            if starting:
                if phase == 0:
                    @pl.when((oa > 0) | (zl != z))
                    def _():
                        arrived(m, pos, z, c)
                else:
                    arrived(m, pos, z, c)

            def send(which, target):
                do(block_copy(m, pos, z, c, send_sem.at[m, pos, z, which], target), starting)

            if phase == 0:
                send(1, neighbour(m, 0, 1))
                send(2, neighbour(m, 0, -1))
                up = (oa == 0) if z == 0 else ((oa == 0) | (oa == 2))
                down = ((oa == 0) | (oa == 1)) if z == 0 else (oa == 0)

                @pl.when(up)
                def _():
                    send(3, neighbour(m, 1, 0))

                @pl.when(down)
                def _():
                    send(4, neighbour(m, -1, 0))
            elif phase == 1:
                if z == 0:
                    @pl.when(ob == 1)
                    def _():
                        send(2, neighbour(m, 0, -1))
                else:
                    @pl.when(ob == 2)
                    def _():
                        send(1, neighbour(m, 0, 1))
            send(0, sibling)

    row = lax.broadcasted_iota(jnp.int32, (PIECE, 1), 0)
    row_a = (row // PAD) * ROWS + row % PAD

    def part_copy(m, pos, yy, xx):
        return pltpu.make_async_remote_copy(
            src_ref=stage.at[m, pos], dst_ref=inbox.at[m, xx, r],
            send_sem=part_send.at[m, pos], recv_sem=part_recv.at[m, xx, r],
            device_id=(g, yy), device_id_type=MESH,
        )

    def compute(m, ob, oa):
        yy, xx = place(m, ob, oa)
        pos = yy * RING + xx
        for z in range(2):
            arrived(m, pos, z, 1 - c)
        first = pos * (QUAD * ROWS)
        last = first + QUAD * ROWS - 1
        low = jnp.int32(-1)
        high = jnp.int32(-1)
        offset = jnp.int32(0)
        edge = jnp.int32(0)
        for h in range(NIRREP):
            low = low + (offset <= first).astype(jnp.int32)
            high = high + (offset <= last).astype(jnp.int32)
            edge = jnp.where(offset <= last, offset, edge)
            offset = offset + virt_ref[h]
        occ = slab_ref[m] // (O // NIRREP)
        pair_low = low ^ occ
        pair_high = high ^ occ
        acc_low = jnp.zeros((PIECE, Q), jnp.float32)
        acc_high = jnp.zeros((PIECE, Q), jnp.float32)
        for k in range(0, K, DEPTH):
            left = buf[m, pos, :, :, k:k + DEPTH].reshape(PIECE, DEPTH)
            for which in range(2):
                right = w_ref[pair_high if which else pair_low, :, k:k + DEPTH]
                term = lax.dot_general(left, right, (((1,), (1,)), ((), ())), preferred_element_type=jnp.float32)
                if which:
                    acc_high = acc_high + term
                else:
                    acc_low = acc_low + term
        stage[m, pos] = encode(jnp.where(row_a + first >= edge, acc_high, acc_low), wide)

        @pl.when(yy != r)
        def _():
            part_copy(m, pos, yy, xx).start()

    def part_sent(m, ob, oa):
        yy, xx = place(m, ob, oa)

        @pl.when(yy != r)
        def _():
            part_copy(m, yy * RING + xx, yy, xx).wait_send()

    def sum_copy(m, xx, s):
        return pltpu.make_async_remote_copy(
            src_ref=total.at[m, xx, pl.ds(s * PAD, PAD)], dst_ref=final.at[m, g % 16],
            send_sem=sum_send.at[m, xx, s], recv_sem=sum_recv.at[m, g % 16],
            device_id=((r * RING + xx) * 4 + s, y), device_id_type=MESH,
        )

    def reduce(m, ob, oa):
        yy, xx = place(m, ob, oa)

        @pl.when(yy == r)
        def _():
            value = decode(stage[m, yy * RING + xx])
            for d in (1, 2, 3):
                src = (r + d) % 4
                pltpu.make_async_remote_copy(
                    src_ref=stage.at[m, 0], dst_ref=inbox.at[m, xx, src],
                    send_sem=part_send.at[m, 0], recv_sem=part_recv.at[m, xx, src],
                    device_id=(g, src), device_id_type=MESH,
                ).wait_recv()
                value = value + decode(inbox[m, xx, src])
            total[m, xx] = encode(value[:, :Q], wide)

            def ship(s, _):
                here = (y == r) & ((r * RING + xx) * 4 + s == g)

                @pl.when(here)
                def _():
                    final[m, g % 16] = total[m, xx, pl.ds(pl.multiple_of(s * PAD, PAD), PAD)]

                @pl.when(jnp.logical_not(here))
                def _():
                    sum_copy(m, xx, s).start()
                return 0

            lax.fori_loop(0, QUAD, ship, 0)

    for m in range(2):
        own_pair(m, True)

    def phase0(oa, _):
        for m in range(2):
            relay(m, 0, oa, 0, True)
        return 0

    lax.fori_loop(0, 4, phase0, 0)
    pl.semaphore_wait(step_sem, 2)
    for d in (1, 3):
        pl.semaphore_signal(far_sem, inc=1, device_id=(g, (r + d) % 4), device_id_type=MESH)
    w_copy.wait()
    pl.semaphore_wait(far_sem, 2)

    def reduce1(i):
        reduce(i % 2, 0, i // 2)
        for m in range(2):
            reduce(m, 1 + i % 2, i // 2)

    def phase1(i, _):
        ob, oa = 1 + i % 2, i // 2
        for m in range(2):
            relay(m, ob, oa, 1, True)

        @pl.when(i >= 2)
        def _():
            reduce1(i - 2)

        compute(i % 2, 0, i // 2)
        for m in range(2):
            compute(m, ob, oa)
        return 0

    lax.fori_loop(0, 8, phase1, 0)

    def phase2(oa, _):
        for m in range(2):
            relay(m, 3, oa, 2, True)

        @pl.when(oa < 2)
        def _():
            reduce1(oa + 6)

        @pl.when(oa >= 2)
        def _():
            for m in range(2):
                reduce(m, 3, oa - 2)

        for m in range(2):
            compute(m, 3, oa)
        return 0

    lax.fori_loop(0, 4, phase2, 0)
    for oa in (2, 3):
        for m in range(2):
            reduce(m, 3, oa)

    def done0(oa, _):
        for m in range(2):
            relay(m, 0, oa, 0, False)
            part_sent(m, 0, oa)
        return 0

    def done1(i, _):
        for m in range(2):
            relay(m, 1 + i % 2, i // 2, 1, False)
            part_sent(m, 1 + i % 2, i // 2)
        return 0

    def done2(oa, _):
        for m in range(2):
            relay(m, 3, oa, 2, False)
            part_sent(m, 3, oa)
        return 0

    for m in range(2):
        own_pair(m, False)
    lax.fori_loop(0, 4, done0, 0)
    lax.fori_loop(0, 8, done1, 0)
    lax.fori_loop(0, 4, done2, 0)

    def landed(k, _):
        @pl.when((y != r) | (r * 16 + k != g))
        def _():
            for m in range(2):
                pltpu.make_async_remote_copy(
                    src_ref=total.at[m, 0, pl.ds(0, PAD)], dst_ref=final.at[m, k],
                    send_sem=sum_send.at[m, 0, 0], recv_sem=sum_recv.at[m, k],
                    device_id=(r * 16 + k, y), device_id_type=MESH,
                ).wait_recv()
        return 0

    lax.fori_loop(0, 16, landed, 0)

    def shipped(t, _):
        xx, s = t // QUAD, t % QUAD

        @pl.when((y != r) | ((r * RING + xx) * 4 + s != g))
        def _():
            for m in range(2):
                sum_copy(m, xx, s).wait_send()
        return 0

    lax.fori_loop(0, 16, shipped, 0)
    for m in range(2):
        for k in range(16):
            out_ref[m, :, k * Q:(k + 1) * Q] = decode(final[m, k])[:ROWS, :Q]


def per_device(amplitudes, integrals, virt_size, slab):
    smem = pl.BlockSpec(memory_space=pltpu.SMEM)
    vmem = pl.BlockSpec(memory_space=pltpu.VMEM)
    dma = pltpu.SemaphoreType.DMA
    return pl.pallas_call(
        kernel,
        out_shape=jax.ShapeDtypeStruct((2, ROWS, K), jnp.float32),
        in_specs=[smem, smem, vmem, pl.BlockSpec(memory_space=pl.ANY)],
        out_specs=vmem,
        scratch_shapes=[
            pltpu.VMEM((2, 16, QUAD, PAD, K), jnp.bfloat16),
            pltpu.VMEM((NIRREP, Q, K), jnp.bfloat16),
            pltpu.VMEM((PIECE, LANES), jnp.float32),
            pltpu.VMEM((2, 16, PIECE, LANES), jnp.int16),
            pltpu.VMEM((2, 4, 4, PIECE, LANES), jnp.int16),
            pltpu.VMEM((2, 4, PIECE, LANES), jnp.int16),
            pltpu.VMEM((2, 16, PAD, LANES), jnp.int16),
            dma,
            dma((2, 16, 4)),
            dma((2, 16, 2, 5)),
            dma((2,)),
            dma((2, 16)),
            dma((2, 4, 4)),
            dma((2, 4, 4)),
            dma((2, 16)),
            pltpu.SemaphoreType.REGULAR,
            pltpu.SemaphoreType.REGULAR,
        ],
        compiler_params=pltpu.CompilerParams(
            collective_id=0, has_side_effects=True, vmem_limit_bytes=56 * 1024 * 1024
        ),
        cost_estimate=pl.CostEstimate(flops=4_600_000_000, bytes_accessed=12_000_000, transcendentals=0),
    )(slab, virt_size, amplitudes, integrals)


def solution(mesh):
    return jax.shard_map(
        per_device,
        mesh=mesh,
        in_specs=(P(None, "grid", "rep"), P(None, "grid", "rep"), P(), P()),
        out_specs=P(None, "grid", "rep"),
        check_vma=False,
    )
```

time: 574 us -> 115 us (0.20)
  local copies, waits for them, and re-layouts: 243 us -> 3.63 us
  waiting for transfers between devices: 217 us -> 0 us
  Pallas kernels: 0 us -> 111 us
  between operations: 42.6 us -> 0.01 us
  matrix products: 36.2 us -> 0 us
  blocking collectives: 30 us -> 0 us
    unnamed x36 -> x1, local copies, waits for them, and re-layouts: 156 us -> 1.62 us
    unnamed x3 -> x0, waiting for transfers between devices: 127 us -> none
    pallas_call x0 -> x1, Pallas kernels: none -> 111 us  [per_device(): pl.pallas_call(kernel, out_shape=jax.ShapeDtypeStruct((2, ROWS, K), jnp.f...]
    all_gather x1 -> x0, waiting for transfers between devices: 90.1 us -> none  [per_device(): whole = lax.all_gather(amplitudes, 'grid', axis=1, tiled=True)]
    dynamic_slice x1 -> x0, local copies, waits for them, and re-layouts: 50.9 us -> none  [accumulate(): lax.dynamic_slice_in_dim(whole[member], anchors[irrep_a], window, 0)]
    dot_general x16 -> x0, matrix products: 36.2 us -> none  [accumulate(): lax.dot_general(window_rows, block_w, (((1,), (1,)), ((), ())), preferred...]
    all_to_all x1 -> x0, blocking collectives: 30 us -> none  [per_device(): lax.all_to_all(partial_value, 'grid', split_axis=1, concat_axis=2, tiled=...]
    slice x3 -> x0, local copies, waits for them, and re-layouts: 23.7 us -> none  [the longest x1 22.4 us: accumulate(): whole[member]]
  transfers between devices with their start and end apart: 2 -> 0, of which waited for: 2 -> 0; matrix products, arithmetic and copies ran while one was open for 1% -> 0% of each run, Pallas kernels for 0% -> 0%
where the time goes in v1:
time: 115 us; the launch traced here: 114 us
  Pallas kernels  111 us (97%)
  local copies, waits for them, and re-layouts  3.63 us (3%)
    pallas_call x1, Pallas kernels, per_device(): pl.pallas_call(kernel, out_shape=jax.ShapeDtypeStruct((2, ROWS, K), jnp.f...  111 us

profile of v1, /device:TPU:16, one launch (start us, length us, event | category | flops | bytes accessed | tf_op | source)
XLA Modules:
  0.0 114.2 jit_solution(10353326437185481798)
XLA Ops:
  0.0 1.6 %copy.5.amp_ref = bf16[2,13,3328]{2,1,0:T(8,128)(2,1)} copy(bf16[2,13,3328]{2,0,1:T(2,128)(2,1)} %param.4) | data formatting | bytes 346112 | tf_op args[0]
  1.6 110.6 %shard_map.46 = f32[2,13,3328]{2,1,0:T(8,128)} custom-call(s32[2]{0:T(128)} %slab_ref.1, s32[8]{0:T(128)} %virt_ref.1, bf16[2,13,3328]{2,1,0:T(8,128)(2,1)} %copy.5.amp_ref, bf16[8,208,3328]{2,1,0:T(8,128)(2,1)} %w_hbm.1), custom_call_target="tpu_custom_call" | custom-call | flops 4600000000 | bytes 12000000 | tf_op jit(solution)/shard_map/pallas_call | solution.py:358
  112.2 2.0 %copy.6 = f32[2,13,3328]{2,0,1:T(2,128)} copy(f32[2,13,3328]{2,1,0:T(8,128)} %shard_map.46) | data formatting | bytes 692224 | tf_op jit(solution)/shard_map/pallas_call | solution.py:358

commit v2 on v0

v2 whole, which is shorter than its diff:
```python
import jax
import jax.numpy as jnp
from jax import lax
from jax.experimental import pallas as pl
from jax.experimental.pallas import tpu as pltpu
from jax.sharding import PartitionSpec as P

NIRREP = 8
O = 128
RING = 4
K = 3328
Q = 208
ROWS = 13
PAD = 16
QUAD = 4
PIECE = QUAD * PAD
LANES = 256
DEPTH = 256
MAIN = 2816
TAIL = K - MAIN
SPARE = PAD - ROWS
FOLDS = 5
STEPS = 32700.0
TURN = (0, 1, 3, 2)
MESH = pl.DeviceIdType.MESH


def encode(value, wide):
    peak = jnp.max(jnp.abs(value), axis=1, keepdims=True)
    level = jnp.ceil(jnp.log2(jnp.maximum(peak, 1e-30)) + 0.01)
    wide[:, :Q] = jnp.round(value * (jnp.exp2(-level) * STEPS))
    wide[:, Q:] = jnp.broadcast_to(level, (value.shape[0], LANES - Q))
    return wide[...].astype(jnp.int32).astype(jnp.int16)


def decode(coded):
    value = coded.astype(jnp.int32).astype(jnp.float32)
    return value * (jnp.exp2(value[:, Q:Q + 1]) * (1.0 / STEPS))


def kernel(
    slab_ref, virt_ref, amp_ref, w_hbm, out_ref,
    buf, w_ref, fold, tail, wide, stage, inbox, total, final, low_tab, high_tab, edge_tab,
    w_sem, recv_sem, side_sem, side_send, major_send, minor_send, extra_send,
    part_send, part_recv, sum_send, sum_recv, step_sem, far_sem,
):
    g = lax.axis_index("grid")
    r = lax.axis_index("rep")
    c = lax.rem(g, 2)
    zl = lax.rem(lax.div(g, 2), 2)
    x = lax.rem(lax.div(g, 4), RING)
    y = lax.div(g, 16)
    within = lax.rem(g, 16)
    xs = [lax.rem(x + d, RING) for d in range(RING)]
    ys = [lax.rem(y + d, RING) for d in range(RING)]

    def grid_of(yy, xx, zz, cc):
        return ((yy * RING + xx) * 2 + zz) * 2 + cc

    x_up, x_down = grid_of(y, xs[1], zl, c), grid_of(y, xs[3], zl, c)
    y_up, y_down = grid_of(ys[1], x, zl, c), grid_of(ys[3], x, zl, c)
    sibling = grid_of(y, x, zl, 1 - c)
    partner = grid_of(y, x, 1 - zl, c)
    beyond = (grid_of(y, x, 1 - zl, c), lax.rem(r + 2 * zl + 3, 4))
    minor_up, minor_down = (x_up, y_up), (x_down, y_down)
    major_up, major_down = (y_up, x_up), (y_down, x_down)
    mine = y * RING + x

    barrier = pltpu.get_barrier_semaphore()
    near = [sibling, partner, x_up, x_down, y_up, y_down]
    for n in near:
        pl.semaphore_signal(barrier, inc=1, device_id=(n, r), device_id_type=MESH)
    pl.semaphore_signal(barrier, inc=1, device_id=beyond, device_id_type=MESH)

    w_copy = pltpu.make_async_copy(w_hbm, w_ref, w_sem)
    w_copy.start()
    for m in range(2):
        whole = amp_ref[:, m, :].astype(jnp.float32)
        fold[:ROWS, :] = whole[:, :MAIN]
        fold[ROWS:, FOLDS * TAIL:] = jnp.zeros((SPARE, MAIN - FOLDS * TAIL), jnp.float32)
        fold[ROWS + 1:, (FOLDS - 1) * TAIL:FOLDS * TAIL] = jnp.zeros((SPARE - 1, TAIL), jnp.float32)
        for j in range(FOLDS):
            n = min(SPARE, ROWS - SPARE * j)
            fold[ROWS:ROWS + n, j * TAIL:(j + 1) * TAIL] = whole[SPARE * j:SPARE * j + n, MAIN:]
        buf[m, mine, zl * 2 + c] = fold[...].astype(jnp.bfloat16)
    tail[...] = jnp.zeros_like(tail)

    def table(pos, _):
        first = pos * (QUAD * ROWS)
        last = first + QUAD * ROWS - 1
        low = jnp.int32(-1)
        high = jnp.int32(-1)
        offset = jnp.int32(0)
        edge = jnp.int32(0)
        for h in range(NIRREP):
            low = low + (offset <= first).astype(jnp.int32)
            high = high + (offset <= last).astype(jnp.int32)
            edge = jnp.where(offset <= last, offset, edge)
            offset = offset + virt_ref[h]
        low_tab[pos] = low
        high_tab[pos] = high
        edge_tab[pos] = edge - first
        return 0

    lax.fori_loop(0, 16, table, 0)
    occ = [slab_ref[m] // (O // NIRREP) for m in range(2)]

    pl.semaphore_wait(barrier, len(near) + 1)

    def block_copy(m, pos, z, cc, send, recv, target):
        block = buf.at[m, pos, z * 2 + cc]
        return pltpu.make_async_remote_copy(
            src_ref=block, dst_ref=block, send_sem=send, recv_sem=recv,
            device_id=(target, r), device_id_type=MESH,
        )

    def push(m, pos, z, sem, target):
        block_copy(m, pos, z, c, sem.at[m], recv_sem.at[m, pos, z], target).start()

    def cross(m, pos, z):
        block_copy(m, pos, z, c, side_send.at[m], side_sem.at[m, pos], sibling).start()

    def arrived(m, pos, z):
        block_copy(m, pos, z, c, side_send.at[m], recv_sem.at[m, pos, z], sibling).wait_recv()

    def spread(m, pos, z):
        push(m, pos, z, major_send, major_up[m])
        push(m, pos, z, major_send, major_down[m])

    def place(m, tb, pa):
        return (ys[tb], pa) if m == 0 else (pa, xs[tb])

    def where(m, tb, pa):
        yy, xx = place(m, tb, pa)
        return yy * RING + xx

    along = (xs, ys)
    for m in range(2):
        push(m, mine, zl, extra_send, partner)
    for m in range(2):
        push(m, mine, zl, minor_send, minor_up[m])
        push(m, mine, zl, minor_send, minor_down[m])
        spread(m, mine, zl)
        cross(m, mine, zl)
    pl.semaphore_signal(step_sem, inc=1, device_id=(partner, r), device_id_type=MESH)
    pl.semaphore_signal(step_sem, inc=1, device_id=beyond, device_id_type=MESH)
    for m in range(2):
        arrived(m, mine, 1 - zl)
        push(m, mine, 1 - zl, minor_send, minor_up[m])
        push(m, mine, 1 - zl, minor_send, minor_down[m])
        spread(m, mine, 1 - zl)
        cross(m, mine, 1 - zl)
    for z in range(2):
        for d in ((1, 3) if z == 0 else (3, 1)):
            for m in range(2):
                pos = where(m, 0, along[m][d])
                arrived(m, pos, z)
                if z == 0 and d == 1:
                    push(m, pos, z, extra_send, minor_down[m])
                if z == 1 and d == 3:
                    push(m, pos, z, extra_send, minor_up[m])
                spread(m, pos, z)
                cross(m, pos, z)
    for z in range(2):
        for m in range(2):
            pos = where(m, 0, along[m][2])
            arrived(m, pos, z)
            spread(m, pos, z)
            cross(m, pos, z)
    pl.semaphore_wait(step_sem, 2)
    for d in (1, 3):
        pl.semaphore_signal(far_sem, inc=1, device_id=(g, lax.rem(r + d, 4)), device_id_type=MESH)
    w_copy.wait()
    pl.semaphore_wait(far_sem, 2)

    row = lax.broadcasted_iota(jnp.int32, (PIECE, 1), 0)
    row_a = (row // PAD) * ROWS + row % PAD

    def part_copy(m, pos, yy, xx):
        return pltpu.make_async_remote_copy(
            src_ref=stage.at[m, pos], dst_ref=inbox.at[m, xx, r],
            send_sem=part_send.at[m], recv_sem=part_recv.at[m, xx],
            device_id=(g, yy), device_id_type=MESH,
        )

    def compute(m, tb, pa):
        yy, xx = place(m, tb, pa)
        pos = yy * RING + xx
        both = buf.at[m, pos, pl.ds(0, 2)]
        pltpu.make_async_remote_copy(
            src_ref=both, dst_ref=both, send_sem=side_send.at[m], recv_sem=side_sem.at[m, pos],
            device_id=(sibling, r), device_id_type=MESH,
        ).wait_recv()
        pair_low = low_tab[pos] ^ occ[m]
        pair_high = high_tab[pos] ^ occ[m]
        edge = edge_tab[pos]
        for s in range(QUAD):
            spill = buf[m, pos, s, :, :FOLDS * TAIL].astype(jnp.float32)
            for j in range(FOLDS):
                n = min(SPARE, ROWS - SPARE * j)
                start = s * PAD + SPARE * j
                tail[start:start + n, :] = spill[ROWS:ROWS + n, j * TAIL:(j + 1) * TAIL]
        acc_low = jnp.zeros((PIECE, Q), jnp.float32)
        acc_high = jnp.zeros((PIECE, Q), jnp.float32)
        for k in range(0, K, DEPTH):
            if k < MAIN:
                left = buf[m, pos, :, :, k:k + DEPTH].reshape(PIECE, DEPTH)
            else:
                left = tail[:, k - MAIN:k - MAIN + DEPTH].astype(jnp.bfloat16)
            for which in range(2):
                right = w_ref[pair_high if which else pair_low, :, k:k + DEPTH]
                term = lax.dot_general(left, right, (((1,), (1,)), ((), ())), preferred_element_type=jnp.float32)
                if which:
                    acc_high = acc_high + term
                else:
                    acc_low = acc_low + term
        stage[m, pos] = encode(jnp.where(row_a >= edge, acc_high, acc_low), wide)

        @pl.when(yy != r)
        def _():
            part_copy(m, pos, yy, xx).start()

    def sum_copy(m, xx, s):
        return pltpu.make_async_remote_copy(
            src_ref=total.at[m, xx, pl.ds(s * PAD, PAD)], dst_ref=final.at[m, within],
            send_sem=sum_send.at[m, xx], recv_sem=sum_recv.at[m],
            device_id=((r * RING + xx) * 4 + s, y), device_id_type=MESH,
        )

    def reduce(m, tb, pa):
        yy, xx = place(m, tb, pa)

        @pl.when(yy == r)
        def _():
            three = inbox.at[m, xx, pl.ds(0, 3)]
            pltpu.make_async_remote_copy(
                src_ref=three, dst_ref=three, send_sem=part_send.at[m], recv_sem=part_recv.at[m, xx],
                device_id=(g, lax.rem(r + 1, 4)), device_id_type=MESH,
            ).wait_recv()
            value = decode(stage[m, yy * RING + xx])
            for d in (1, 2, 3):
                value = value + decode(inbox[m, xx, lax.rem(r + d, 4)])
            total[m, xx] = encode(value[:, :Q], wide)

            def ship(s, _):
                here = (y == r) & ((r * RING + xx) * 4 + s == g)

                @pl.when(here)
                def _():
                    final[m, within] = total[m, xx, pl.ds(pl.multiple_of(s * PAD, PAD), PAD)]

                @pl.when(jnp.logical_not(here))
                def _():
                    sum_copy(m, xx, s).start()
                return 0

            lax.fori_loop(0, QUAD, ship, 0)

    def relay(m, tb, pa):
        pos = where(m, tb, pa)
        for z in ((1, 0) if tb == 3 else (0, 1)):
            arrived(m, pos, z)
            if tb == 1 and z == 0:
                push(m, pos, z, major_send, major_down[m])
            if tb == 3 and z == 1:
                push(m, pos, z, major_send, major_up[m])
            cross(m, pos, z)

    def spots(oa):
        t = oa + lax.div(oa, 2) - 2 * lax.div(oa, 3)
        return lax.rem(x + t, RING), lax.rem(y + t, RING)

    def phase1(oa, _):
        pa = spots(oa)
        relay(0, 1, pa[0])
        compute(0, 0, pa[0])
        relay(1, 1, pa[1])
        relay(0, 3, pa[0])
        compute(1, 0, pa[1])
        relay(1, 3, pa[1])
        compute(0, 1, pa[0])
        compute(1, 1, pa[1])
        compute(0, 3, pa[0])
        compute(1, 3, pa[1])
        return 0

    lax.fori_loop(0, 4, phase1, 0)

    def phase2(oa, _):
        pa = spots(oa)
        relay(0, 2, pa[0])
        relay(1, 2, pa[1])
        for m in range(2):
            compute(m, 2, pa[m])
            for tb in (0, 1, 3):
                reduce(m, tb, pa[m])
        return 0

    lax.fori_loop(0, 4, phase2, 0)

    def finish(oa, _):
        pa = spots(oa)
        for m in range(2):
            reduce(m, 2, pa[m])
        return 0

    lax.fori_loop(0, 4, finish, 0)

    def wait_sent(ref, sem):
        pltpu.make_async_remote_copy(
            src_ref=ref, dst_ref=ref, send_sem=sem, recv_sem=sum_recv.at[0],
            device_id=(sibling, r), device_id_type=MESH,
        ).wait_send()

    for m in range(2):
        wait_sent(buf.at[m, pl.ds(0, 8)], side_send.at[m])
        wait_sent(buf.at[m, pl.ds(0, 6)], major_send.at[m])
        wait_sent(buf.at[m, 0], minor_send.at[m])
        wait_sent(buf.at[m, 0, pl.ds(0, 3)], extra_send.at[m])
        wait_sent(stage.at[m, pl.ds(0, 12)], part_send.at[m])
        for xx in range(RING):
            inside = (y == r) & (x == xx)

            @pl.when(inside)
            def _():
                wait_sent(total.at[m, xx, pl.ds(0, PIECE - PAD)], sum_send.at[m, xx])

            @pl.when(jnp.logical_not(inside))
            def _():
                wait_sent(total.at[m, xx], sum_send.at[m, xx])

        def landed(ref):
            pltpu.make_async_remote_copy(
                src_ref=ref, dst_ref=ref, send_sem=sum_send.at[m, 0], recv_sem=sum_recv.at[m],
                device_id=(sibling, r), device_id_type=MESH,
            ).wait_recv()

        @pl.when(y == r)
        def _():
            landed(final.at[m, pl.ds(0, 15)])

        @pl.when(y != r)
        def _():
            landed(final.at[m])
        for k in range(16):
            out_ref[:, m, k * Q:(k + 1) * Q] = decode(final[m, k])[:ROWS, :Q]


def per_device(amplitudes, integrals, virt_size, slab):
    smem = pl.BlockSpec(memory_space=pltpu.SMEM)
    vmem = pl.BlockSpec(memory_space=pltpu.VMEM)
    dma = pltpu.SemaphoreType.DMA
    out = pl.pallas_call(
        kernel,
        out_shape=jax.ShapeDtypeStruct((ROWS, 2, K), jnp.float32),
        in_specs=[smem, smem, vmem, pl.BlockSpec(memory_space=pl.ANY)],
        out_specs=vmem,
        scratch_shapes=[
            pltpu.VMEM((2, 16, QUAD, PAD, MAIN), jnp.bfloat16),
            pltpu.VMEM((NIRREP, Q, K), jnp.bfloat16),
            pltpu.VMEM((PAD, MAIN), jnp.float32),
            pltpu.VMEM((PIECE, TAIL), jnp.float32),
            pltpu.VMEM((PIECE, LANES), jnp.float32),
            pltpu.VMEM((2, 16, PIECE, LANES), jnp.int16),
            pltpu.VMEM((2, 4, 4, PIECE, LANES), jnp.int16),
            pltpu.VMEM((2, 4, PIECE, LANES), jnp.int16),
            pltpu.VMEM((2, 16, PAD, LANES), jnp.int16),
            pltpu.SMEM((16,), jnp.int32),
            pltpu.SMEM((16,), jnp.int32),
            pltpu.SMEM((16,), jnp.int32),
            dma,
            dma((2, 16, 2)),
            dma((2, 16)),
            dma((2,)),
            dma((2,)),
            dma((2,)),
            dma((2,)),
            dma((2,)),
            dma((2, 4)),
            dma((2, 4)),
            dma((2,)),
            pltpu.SemaphoreType.REGULAR,
            pltpu.SemaphoreType.REGULAR,
        ],
        compiler_params=pltpu.CompilerParams(
            collective_id=0, has_side_effects=True, vmem_limit_bytes=56 * 1024 * 1024
        ),
        cost_estimate=pl.CostEstimate(flops=4_600_000_000, bytes_accessed=12_000_000, transcendentals=0),
    )(slab, virt_size, jnp.transpose(amplitudes, (1, 0, 2)), integrals)
    return jnp.transpose(out, (1, 0, 2))


def solution(mesh):
    return jax.shard_map(
        per_device,
        mesh=mesh,
        in_specs=(P(None, "grid", "rep"), P(None, "grid", "rep"), P(), P()),
        out_specs=P(None, "grid", "rep"),
        check_vma=False,
    )
```

time: 574 us -> 89.3 us (0.16)
  local copies, waits for them, and re-layouts: 243 us -> 1.74 us
  waiting for transfers between devices: 217 us -> 0 us
  Pallas kernels: 0 us -> 86.9 us
  between operations: 42.6 us -> 0.01 us
  matrix products: 36.2 us -> 0 us
  blocking collectives: 30 us -> 0 us
    unnamed x36 -> x1, local copies, waits for them, and re-layouts: 156 us -> 1.74 us
    unnamed x3 -> x0, waiting for transfers between devices: 127 us -> none
    all_gather x1 -> x0, waiting for transfers between devices: 90.1 us -> none  [per_device(): whole = lax.all_gather(amplitudes, 'grid', axis=1, tiled=True)]
    pallas_call x0 -> x1, Pallas kernels: none -> 86.9 us  [per_device(): pl.pallas_call(kernel, out_shape=jax.ShapeDtypeStruct((ROWS, 2, K), jnp.f...]
    dynamic_slice x1 -> x0, local copies, waits for them, and re-layouts: 50.9 us -> none  [accumulate(): lax.dynamic_slice_in_dim(whole[member], anchors[irrep_a], window, 0)]
    dot_general x16 -> x0, matrix products: 36.2 us -> none  [accumulate(): lax.dot_general(window_rows, block_w, (((1,), (1,)), ((), ())), preferred...]
    all_to_all x1 -> x0, blocking collectives: 30 us -> none  [per_device(): lax.all_to_all(partial_value, 'grid', split_axis=1, concat_axis=2, tiled=...]
    slice x3 -> x0, local copies, waits for them, and re-layouts: 23.7 us -> none  [the longest x1 22.4 us: accumulate(): whole[member]]
  transfers between devices with their start and end apart: 2 -> 0, of which waited for: 2 -> 0; matrix products, arithmetic and copies ran while one was open for 1% -> 0% of each run, Pallas kernels for 0% -> 0%
where the time goes in v2:
time: 89.3 us; the launch traced here: 88.7 us
  Pallas kernels  86.9 us (97%)
  local copies, waits for them, and re-layouts  1.74 us (2%)
    pallas_call x1, Pallas kernels, per_device(): pl.pallas_call(kernel, out_shape=jax.ShapeDtypeStruct((ROWS, 2, K), jnp.f...  86.9 us

profile of v2, /device:TPU:16, one launch (start us, length us, event | category | flops | bytes accessed | tf_op | source)
XLA Modules:
  0.0 88.7 jit_solution(8020018889159690108)
XLA Ops:
  0.0 86.9 %shard_map.46 = f32[13,2,3328]{2,1,0:T(2,128)} custom-call(s32[2]{0:T(128)} %slab_ref.1, s32[8]{0:T(128)} %virt_ref.1, bf16[13,2,3328]{2,1,0:T(2,128)(2,1)} %bitcast.3, bf16[8,208,3328]{2,1,0:T(8,128)(2,1)} %w_hbm.1), custom_call_target="tpu_custom_call" | custom-call | flops 4600000000 | bytes 12000000 | tf_op jit(solution)/shard_map/pallas_call | solution.py:353
  86.9 1.7 %copy.6 = f32[2,13,3328]{2,0,1:T(2,128)} copy(f32[2,13,3328]{2,0,1:T(2,128)} %bitcast.2) | data formatting | bytes 692224

commit v3 on v2

v3 whole, which is shorter than its diff:
```python
import jax
import jax.numpy as jnp
from jax import lax
from jax.experimental import pallas as pl
from jax.experimental.pallas import tpu as pltpu
from jax.sharding import PartitionSpec as P

NIRREP = 8
O = 128
RING = 4
K = 3328
Q = 208
ROWS = 13
PAD = 16
QUAD = 4
PIECE = QUAD * PAD
LANES = 256
DEPTH = 256
MAIN = 2816
TAIL = K - MAIN
SPARE = PAD - ROWS
FOLDS = 5
STEPS = 32700.0
LAG = 4
MESH = pl.DeviceIdType.MESH


def encode(value, wide):
    peak = jnp.max(jnp.abs(value), axis=1, keepdims=True)
    level = jnp.ceil(jnp.log2(jnp.maximum(peak, 1e-30)) + 0.01)
    wide[:, :Q] = jnp.round(value * (jnp.exp2(-level) * STEPS))
    wide[:, Q:] = jnp.broadcast_to(level, (value.shape[0], LANES - Q))
    return wide[...].astype(jnp.int32).astype(jnp.int16)


def decode(coded):
    value = coded.astype(jnp.int32).astype(jnp.float32)
    return value * (jnp.exp2(value[:, Q:Q + 1]) * (1.0 / STEPS))


def kernel(
    slab_ref, virt_ref, amp_ref, w_hbm, out_ref,
    buf, w_ref, fold, tail, wide, stage, inbox, total, final, low_tab, high_tab, edge_tab,
    w_sem, recv_sem, side_sem, side_send, major_send, minor_send, extra_send,
    part_send, part_recv, sum_send, sum_recv, step_sem, far_sem,
):
    g = lax.axis_index("grid")
    r = lax.axis_index("rep")
    c = lax.rem(g, 2)
    zl = lax.rem(lax.div(g, 2), 2)
    x = lax.rem(lax.div(g, 4), RING)
    y = lax.div(g, 16)
    within = lax.rem(g, 16)
    xs = [lax.rem(x + d, RING) for d in range(RING)]
    ys = [lax.rem(y + d, RING) for d in range(RING)]

    def grid_of(yy, xx, zz, cc):
        return ((yy * RING + xx) * 2 + zz) * 2 + cc

    x_up, x_down = grid_of(y, xs[1], zl, c), grid_of(y, xs[3], zl, c)
    y_up, y_down = grid_of(ys[1], x, zl, c), grid_of(ys[3], x, zl, c)
    sibling = grid_of(y, x, zl, 1 - c)
    partner = grid_of(y, x, 1 - zl, c)
    beyond = (grid_of(y, x, 1 - zl, c), lax.rem(r + 2 * zl + 3, 4))
    minor_up, minor_down = (x_up, y_up), (x_down, y_down)
    major_up, major_down = (y_up, x_up), (y_down, x_down)
    mine = y * RING + x

    barrier = pltpu.get_barrier_semaphore()
    near = [sibling, partner, x_up, x_down, y_up, y_down]
    for n in near:
        pl.semaphore_signal(barrier, inc=1, device_id=(n, r), device_id_type=MESH)
    pl.semaphore_signal(barrier, inc=1, device_id=beyond, device_id_type=MESH)

    w_copy = pltpu.make_async_copy(w_hbm, w_ref, w_sem)
    w_copy.start()
    for m in range(2):
        whole = amp_ref[:, m, :].astype(jnp.float32)
        fold[:ROWS, :] = whole[:, :MAIN]
        fold[ROWS:, FOLDS * TAIL:] = jnp.zeros((SPARE, MAIN - FOLDS * TAIL), jnp.float32)
        fold[ROWS + 1:, (FOLDS - 1) * TAIL:FOLDS * TAIL] = jnp.zeros((SPARE - 1, TAIL), jnp.float32)
        for j in range(FOLDS):
            n = min(SPARE, ROWS - SPARE * j)
            fold[ROWS:ROWS + n, j * TAIL:(j + 1) * TAIL] = whole[SPARE * j:SPARE * j + n, MAIN:]
        buf[m, mine, c * 2 + zl] = fold[...].astype(jnp.bfloat16)
    tail[...] = jnp.zeros_like(tail)

    def table(pos, _):
        first = pos * (QUAD * ROWS)
        last = first + QUAD * ROWS - 1
        low = jnp.int32(-1)
        high = jnp.int32(-1)
        offset = jnp.int32(0)
        edge = jnp.int32(0)
        for h in range(NIRREP):
            low = low + (offset <= first).astype(jnp.int32)
            high = high + (offset <= last).astype(jnp.int32)
            edge = jnp.where(offset <= last, offset, edge)
            offset = offset + virt_ref[h]
        low_tab[pos] = low
        high_tab[pos] = high
        edge_tab[pos] = edge - first
        return 0

    lax.fori_loop(0, 16, table, 0)
    occ = [slab_ref[m] // (O // NIRREP) for m in range(2)]

    pl.semaphore_wait(barrier, len(near) + 1)

    def block_copy(m, pos, z, send, recv, target):
        block = buf.at[m, pos, pl.ds(2 * c, 2)] if z is None else buf.at[m, pos, c * 2 + z]
        return pltpu.make_async_remote_copy(
            src_ref=block, dst_ref=block, send_sem=send, recv_sem=recv,
            device_id=(target, r), device_id_type=MESH,
        )

    def push(m, pos, z, sem, target):
        block_copy(m, pos, z, sem.at[m], recv_sem.at[m, pos], target).start()

    def cross(m, pos):
        block_copy(m, pos, None, side_send.at[m], side_sem.at[m, pos], sibling).start()

    def arrived(m, pos, z):
        block_copy(m, pos, z, side_send.at[m], recv_sem.at[m, pos], sibling).wait_recv()

    def spread(m, pos, z):
        push(m, pos, z, major_send, major_up[m])
        push(m, pos, z, major_send, major_down[m])

    def place(m, tb, ta):
        db, da = (y, x) if m == 0 else (x, y)
        pb, pa = lax.rem(db + tb, RING), lax.rem(da + ta, RING)
        return (pb, pa) if m == 0 else (pa, pb)

    def take(m, tb, ta):
        yy, xx = place(m, tb, ta)
        pos = yy * RING + xx
        arrived(m, pos, None)

        @pl.when(tb == 0)
        def _():
            @pl.when(ta == 1)
            def _():
                push(m, pos, 0, extra_send, minor_down[m])

            @pl.when(ta == 3)
            def _():
                push(m, pos, 1, extra_send, minor_up[m])

            spread(m, pos, None)

        for side, target in ((1, major_down[m]), (3, major_up[m])):
            @pl.when((tb == side) & ((ta == 0) | (ta == 2)))
            def _():
                push(m, pos, side // 2, major_send, target)

            @pl.when((tb == side) & (ta == side))
            def _():
                push(m, pos, None, major_send, target)

        cross(m, pos)

    for m in range(2):
        push(m, mine, zl, extra_send, partner)
    for m in range(2):
        push(m, mine, zl, minor_send, minor_up[m])
        push(m, mine, zl, minor_send, minor_down[m])
        spread(m, mine, zl)
    pl.semaphore_signal(step_sem, inc=1, device_id=(partner, r), device_id_type=MESH)
    pl.semaphore_signal(step_sem, inc=1, device_id=beyond, device_id_type=MESH)
    for m in range(2):
        arrived(m, mine, 1 - zl)
        push(m, mine, 1 - zl, minor_send, minor_up[m])
        push(m, mine, 1 - zl, minor_send, minor_down[m])
        spread(m, mine, 1 - zl)
        cross(m, mine)
    pl.semaphore_wait(step_sem, 2)
    for d in (1, 3):
        pl.semaphore_signal(far_sem, inc=1, device_id=(g, lax.rem(r + d, 4)), device_id_type=MESH)
    w_copy.wait()
    pl.semaphore_wait(far_sem, 2)

    row = lax.broadcasted_iota(jnp.int32, (PIECE, 1), 0)
    part = row // PAD
    row_a = ((part % 2) * 2 + part // 2) * ROWS + row % PAD

    others = [lax.rem(r + d, 4) for d in (1, 2, 3)]

    def send_parts(step):
        for there in others:
            pltpu.make_async_remote_copy(
                src_ref=stage.at[there, pl.ds(2 * step, 2)], dst_ref=inbox.at[r, pl.ds(2 * step, 2)],
                send_sem=part_send, recv_sem=part_recv.at[step],
                device_id=(g, there), device_id_type=MESH,
            ).start()

    def compute(m, tb, ta, t):
        yy, xx = place(m, tb, ta)
        pos = yy * RING + xx
        pair = buf.at[m, pos, pl.ds(0, 2)]
        pltpu.make_async_remote_copy(
            src_ref=pair, dst_ref=pair, send_sem=side_send.at[m], recv_sem=side_sem.at[m, pos],
            device_id=(sibling, r), device_id_type=MESH,
        ).wait_recv()
        pair_low = low_tab[pos] ^ occ[m]
        pair_high = high_tab[pos] ^ occ[m]
        edge = edge_tab[pos]
        for s in range(QUAD):
            spill = buf[m, pos, s, :, :FOLDS * TAIL].astype(jnp.float32)
            for j in range(FOLDS):
                n = min(SPARE, ROWS - SPARE * j)
                start = s * PAD + SPARE * j
                tail[start:start + n, :] = spill[ROWS:ROWS + n, j * TAIL:(j + 1) * TAIL]
        acc_low = jnp.zeros((PIECE, Q), jnp.float32)
        acc_high = jnp.zeros((PIECE, Q), jnp.float32)
        for k in range(0, K, DEPTH):
            if k < MAIN:
                left = buf[m, pos, :, :, k:k + DEPTH].reshape(PIECE, DEPTH)
            else:
                left = tail[:, k - MAIN:k - MAIN + DEPTH].astype(jnp.bfloat16)
            for which in range(2):
                right = w_ref[pair_high if which else pair_low, :, k:k + DEPTH]
                term = lax.dot_general(left, right, (((1,), (1,)), ((), ())), preferred_element_type=jnp.float32)
                if which:
                    acc_high = acc_high + term
                else:
                    acc_low = acc_low + term
        coded = encode(jnp.where(row_a >= edge, acc_high, acc_low), wide.at[pl.ds(0, PIECE)])
        for there in range(4):
            stage[there, t] = coded[there * PAD:(there + 1) * PAD]

    alone = (y == r) & (c * 2 + zl == r)
    seat = lax.rem(r, 2) * 2 + lax.div(r, 2)

    def reduce(step, tb, ta):
        three = inbox.at[0, pl.ds(0, 6)]
        pltpu.make_async_remote_copy(
            src_ref=three, dst_ref=three, send_sem=part_send, recv_sem=part_recv.at[step],
            device_id=(g, others[0]), device_id_type=MESH,
        ).wait_recv()

        def load(ref, k):
            return decode(ref[k, pl.ds(2 * step, 2)].reshape(2 * PAD, LANES))

        value = load(stage, r)
        for there in others:
            value = value + load(inbox, there)
        coded = encode(value[:, :Q], wide.at[pl.ds(0, 2 * PAD)])
        total[pl.ds(2 * step, 2)] = coded.reshape(2, PAD, LANES)
        here = alone & (step == 0)
        for m in range(2):
            yy, xx = place(m, tb, ta)

            @pl.when(here)
            def _():
                final[m, within] = total[2 * step + m]

            @pl.when(jnp.logical_not(here))
            def _():
                pltpu.make_async_remote_copy(
                    src_ref=total.at[2 * step + m], dst_ref=final.at[m, within],
                    send_sem=sum_send.at[m], recv_sem=sum_recv.at[m],
                    device_id=((yy * RING + xx) * 4 + seat, y), device_id_type=MESH,
                ).start()

    order = (
        (0, 0), (0, 1), (0, 3), (1, 0), (3, 0), (0, 2), (1, 1), (3, 3),
        (1, 3), (3, 1), (2, 0), (1, 2), (3, 2), (2, 1), (2, 3), (2, 2),
    )

    def code(k, first, last):
        return sum(order[i][k] * 4 ** (i - first) for i in range(first, last))

    def work(step, state):
        tb, ta, cb, ca = state
        nb, na = lax.rem(cb, 4), lax.rem(ca, 4)
        for m in range(2):
            take(m, nb, na)
            compute(m, tb, ta, 2 * step + m)
        send_parts(step)
        return nb, na, lax.div(cb, 4), lax.div(ca, 4)

    def work_and_reduce(step, states):
        state, (rb, ra) = states
        state = work(step, state)
        reduce(step - LAG, lax.rem(rb, 4), lax.rem(ra, 4))
        return state, (lax.div(rb, 4), lax.div(ra, 4))

    def rest(step, old):
        rb, ra = old
        reduce(step, lax.rem(rb, 4), lax.rem(ra, 4))
        return lax.div(rb, 4), lax.div(ra, 4)

    zero = jnp.int32(0)
    state = (zero, zero, jnp.int32(code(0, 1, 16)), jnp.int32(code(1, 1, 16)))
    old = (jnp.int32(code(0, 0, 15 - LAG)), jnp.int32(code(1, 0, 15 - LAG)))
    state = lax.fori_loop(0, LAG, work, state)
    state, _ = lax.fori_loop(LAG, 15, work_and_reduce, (state, old))
    for m in range(2):
        compute(m, state[0], state[1], 30 + m)
    send_parts(15)
    left = (jnp.int32(code(0, 15 - LAG, 16)), jnp.int32(code(1, 15 - LAG, 16)))
    lax.fori_loop(15 - LAG, 16, rest, left)

    def wait_sent(ref, sem):
        pltpu.make_async_remote_copy(
            src_ref=ref, dst_ref=ref, send_sem=sem, recv_sem=sum_recv.at[0],
            device_id=(sibling, r), device_id_type=MESH,
        ).wait_send()

    wait_sent(stage.at[pl.ds(0, 3)], part_send)
    for m in range(2):
        wait_sent(buf.at[m, pl.ds(0, 8)], side_send.at[m])
        wait_sent(buf.at[m, pl.ds(0, 6)], major_send.at[m])
        wait_sent(buf.at[m, 0], minor_send.at[m])
        wait_sent(buf.at[m, 0, pl.ds(0, 3)], extra_send.at[m])

        def settle(ref):
            copy = pltpu.make_async_remote_copy(
                src_ref=ref, dst_ref=ref, send_sem=sum_send.at[m], recv_sem=sum_recv.at[m],
                device_id=(sibling, r), device_id_type=MESH,
            )
            copy.wait_send()
            copy.wait_recv()

        @pl.when(alone)
        def _():
            settle(final.at[m, pl.ds(0, 15)])

        @pl.when(jnp.logical_not(alone))
        def _():
            settle(final.at[m])
        for k in range(16):
            out_ref[:, m, k * Q:(k + 1) * Q] = decode(final[m, k])[:ROWS, :Q]


def per_device(amplitudes, integrals, virt_size, slab):
    smem = pl.BlockSpec(memory_space=pltpu.SMEM)
    vmem = pl.BlockSpec(memory_space=pltpu.VMEM)
    dma = pltpu.SemaphoreType.DMA
    out = pl.pallas_call(
        kernel,
        out_shape=jax.ShapeDtypeStruct((ROWS, 2, K), jnp.float32),
        in_specs=[smem, smem, vmem, pl.BlockSpec(memory_space=pl.ANY)],
        out_specs=vmem,
        scratch_shapes=[
            pltpu.VMEM((2, 16, QUAD, PAD, MAIN), jnp.bfloat16),
            pltpu.VMEM((NIRREP, Q, K), jnp.bfloat16),
            pltpu.VMEM((PAD, MAIN), jnp.float32),
            pltpu.VMEM((PIECE, TAIL), jnp.float32),
            pltpu.VMEM((PIECE, LANES), jnp.float32),
            pltpu.VMEM((4, 32, PAD, LANES), jnp.int16),
            pltpu.VMEM((4, 32, PAD, LANES), jnp.int16),
            pltpu.VMEM((32, PAD, LANES), jnp.int16),
            pltpu.VMEM((2, 16, PAD, LANES), jnp.int16),
            pltpu.SMEM((16,), jnp.int32),
            pltpu.SMEM((16,), jnp.int32),
            pltpu.SMEM((16,), jnp.int32),
            dma,
            dma((2, 16)),
            dma((2, 16)),
            dma((2,)),
            dma((2,)),
            dma((2,)),
            dma((2,)),
            dma,
            dma((16,)),
            dma((2,)),
            dma((2,)),
            pltpu.SemaphoreType.REGULAR,
            pltpu.SemaphoreType.REGULAR,
        ],
        compiler_params=pltpu.CompilerParams(
            collective_id=0, has_side_effects=True, vmem_limit_bytes=56 * 1024 * 1024
        ),
        cost_estimate=pl.CostEstimate(flops=4_600_000_000, bytes_accessed=12_000_000, transcendentals=0),
    )(slab, virt_size, jnp.transpose(amplitudes, (1, 0, 2)), integrals)
    return jnp.transpose(out, (1, 0, 2))


def solution(mesh):
    return jax.shard_map(
        per_device,
        mesh=mesh,
        in_specs=(P(None, "grid", "rep"), P(None, "grid", "rep"), P(), P()),
        out_specs=P(None, "grid", "rep"),
        check_vma=False,
    )
```

time: 89.3 us -> 79.5 us (0.89)
  Pallas kernels: 86.9 us -> 77.6 us
    pallas_call x1, Pallas kernels: 86.9 us -> 77.6 us  [per_device(): pl.pallas_call(kernel, out_shape=jax.ShapeDtypeStruct((ROWS, 2, K), jnp.f...]
where the time goes in v3:
time: 79.5 us; the launch traced here: 79.4 us
  Pallas kernels  77.6 us (98%)
  local copies, waits for them, and re-layouts  1.74 us (2%)
    pallas_call x1, Pallas kernels, per_device(): pl.pallas_call(kernel, out_shape=jax.ShapeDtypeStruct((ROWS, 2, K), jnp.f...  77.6 us
    unnamed x1, local copies, waits for them, and re-layouts  1.74 us

profile of v3, /device:TPU:16, one launch (start us, length us, event | category | flops | bytes accessed | tf_op | source)
XLA Modules:
  0.0 79.4 jit_solution(13891693139043130154)
XLA Ops:
  0.0 77.6 %shard_map.46 = f32[13,2,3328]{2,1,0:T(2,128)} custom-call(s32[2]{0:T(128)} %slab_ref.1, s32[8]{0:T(128)} %virt_ref.1, bf16[13,2,3328]{2,1,0:T(2,128)(2,1)} %bitcast.3, bf16[8,208,3328]{2,1,0:T(8,128)(2,1)} %w_hbm.1), custom_call_target="tpu_custom_call" | custom-call | flops 4600000000 | bytes 12000000 | tf_op jit(solution)/shard_map/pallas_call | solution.py:341
  77.6 1.7 %copy.6 = f32[2,13,3328]{2,0,1:T(2,128)} copy(f32[2,13,3328]{2,0,1:T(2,128)} %bitcast.2) | data formatting | bytes 692224

commit v4 on v3

--- a/solution.py
+++ b/solution.py
@@ -184,17 +184,14 @@
     part = row // PAD
     row_a = ((part % 2) * 2 + part // 2) * ROWS + row % PAD
 
-    others = [lax.rem(r + d, 4) for d in (1, 2, 3)]
-
-    def send_parts(step):
-        for there in others:
-            pltpu.make_async_remote_copy(
-                src_ref=stage.at[there, pl.ds(2 * step, 2)], dst_ref=inbox.at[r, pl.ds(2 * step, 2)],
-                send_sem=part_send, recv_sem=part_recv.at[step],
-                device_id=(g, there), device_id_type=MESH,
-            ).start()
-
-    def compute(m, tb, ta, t):
+    def part_copy(m, pos, yy, xx):
+        return pltpu.make_async_remote_copy(
+            src_ref=stage.at[m, pos], dst_ref=inbox.at[m, xx, r],
+            send_sem=part_send.at[m], recv_sem=part_recv.at[m, xx],
+            device_id=(g, yy), device_id_type=MESH,
+        )
+
+    def compute(m, tb, ta):
         yy, xx = place(m, tb, ta)
         pos = yy * RING + xx
         pair = buf.at[m, pos, pl.ds(0, 2)]
@@ -225,47 +222,54 @@
                     acc_high = acc_high + term
                 else:
                     acc_low = acc_low + term
-        coded = encode(jnp.where(row_a >= edge, acc_high, acc_low), wide.at[pl.ds(0, PIECE)])
-        for there in range(4):
-            stage[there, t] = coded[there * PAD:(there + 1) * PAD]
-
-    alone = (y == r) & (c * 2 + zl == r)
-    seat = lax.rem(r, 2) * 2 + lax.div(r, 2)
-
-    def reduce(step, tb, ta):
-        three = inbox.at[0, pl.ds(0, 6)]
-        pltpu.make_async_remote_copy(
-            src_ref=three, dst_ref=three, send_sem=part_send, recv_sem=part_recv.at[step],
-            device_id=(g, others[0]), device_id_type=MESH,
-        ).wait_recv()
-
-        def load(ref, k):
-            return decode(ref[k, pl.ds(2 * step, 2)].reshape(2 * PAD, LANES))
-
-        value = load(stage, r)
-        for there in others:
-            value = value + load(inbox, there)
-        coded = encode(value[:, :Q], wide.at[pl.ds(0, 2 * PAD)])
-        total[pl.ds(2 * step, 2)] = coded.reshape(2, PAD, LANES)
-        here = alone & (step == 0)
-        for m in range(2):
-            yy, xx = place(m, tb, ta)
-
-            @pl.when(here)
-            def _():
-                final[m, within] = total[2 * step + m]
-
-            @pl.when(jnp.logical_not(here))
-            def _():
-                pltpu.make_async_remote_copy(
-                    src_ref=total.at[2 * step + m], dst_ref=final.at[m, within],
-                    send_sem=sum_send.at[m], recv_sem=sum_recv.at[m],
-                    device_id=((yy * RING + xx) * 4 + seat, y), device_id_type=MESH,
-                ).start()
+        stage[m, pos] = encode(jnp.where(row_a >= edge, acc_high, acc_low), wide)
+
+        @pl.when(yy != r)
+        def _():
+            part_copy(m, pos, yy, xx).start()
+
+    def seat(s):
+        return lax.rem(s, 2) * 2 + lax.div(s, 2)
+
+    def sum_copy(m, xx, s):
+        return pltpu.make_async_remote_copy(
+            src_ref=total.at[m, xx, pl.ds(s * PAD, PAD)], dst_ref=final.at[m, within],
+            send_sem=sum_send.at[m, xx], recv_sem=sum_recv.at[m],
+            device_id=((r * RING + xx) * 4 + seat(s), y), device_id_type=MESH,
+        )
+
+    def reduce(m, tb, ta):
+        yy, xx = place(m, tb, ta)
+
+        @pl.when(yy == r)
+        def _():
+            three = inbox.at[m, xx, pl.ds(0, 3)]
+            pltpu.make_async_remote_copy(
+                src_ref=three, dst_ref=three, send_sem=part_send.at[m], recv_sem=part_recv.at[m, xx],
+                device_id=(g, lax.rem(r + 1, 4)), device_id_type=MESH,
+            ).wait_recv()
+            value = decode(stage[m, yy * RING + xx])
+            for d in (1, 2, 3):
+                value = value + decode(inbox[m, xx, lax.rem(r + d, 4)])
+            total[m, xx] = encode(value[:, :Q], wide)
+
+            def ship(s, _):
+                here = (y == r) & ((r * RING + xx) * 4 + seat(s) == g)
+
+                @pl.when(here)
+                def _():
+                    final[m, within] = total[m, xx, pl.ds(pl.multiple_of(s * PAD, PAD), PAD)]
+
+                @pl.when(jnp.logical_not(here))
+                def _():
+                    sum_copy(m, xx, s).start()
+                return 0
+
+            lax.fori_loop(0, QUAD, ship, 0)
 
     order = (
-        (0, 0), (0, 1), (0, 3), (1, 0), (3, 0), (0, 2), (1, 1), (3, 3),
-        (1, 3), (3, 1), (2, 0), (1, 2), (3, 2), (2, 1), (2, 3), (2, 2),
+        (0, 0), (0, 1), (0, 3), (1, 0), (3, 0), (0, 2), (2, 0), (1, 1),
+        (3, 3), (1, 3), (3, 1), (1, 2), (3, 2), (2, 1), (2, 3), (2, 2),
     )
 
     def code(k, first, last):
@@ -276,19 +280,20 @@
         nb, na = lax.rem(cb, 4), lax.rem(ca, 4)
         for m in range(2):
             take(m, nb, na)
-            compute(m, tb, ta, 2 * step + m)
-        send_parts(step)
+            compute(m, tb, ta)
         return nb, na, lax.div(cb, 4), lax.div(ca, 4)
 
     def work_and_reduce(step, states):
         state, (rb, ra) = states
         state = work(step, state)
-        reduce(step - LAG, lax.rem(rb, 4), lax.rem(ra, 4))
+        for m in range(2):
+            reduce(m, lax.rem(rb, 4), lax.rem(ra, 4))
         return state, (lax.div(rb, 4), lax.div(ra, 4))
 
     def rest(step, old):
         rb, ra = old
-        reduce(step, lax.rem(rb, 4), lax.rem(ra, 4))
+        for m in range(2):
+            reduce(m, lax.rem(rb, 4), lax.rem(ra, 4))
         return lax.div(rb, 4), lax.div(ra, 4)
 
     zero = jnp.int32(0)
@@ -297,8 +302,7 @@
     state = lax.fori_loop(0, LAG, work, state)
     state, _ = lax.fori_loop(LAG, 15, work_and_reduce, (state, old))
     for m in range(2):
-        compute(m, state[0], state[1], 30 + m)
-    send_parts(15)
+        compute(m, state[0], state[1])
     left = (jnp.int32(code(0, 15 - LAG, 16)), jnp.int32(code(1, 15 - LAG, 16)))
     lax.fori_loop(15 - LAG, 16, rest, left)
 
@@ -308,28 +312,36 @@
             device_id=(sibling, r), device_id_type=MESH,
         ).wait_send()
 
-    wait_sent(stage.at[pl.ds(0, 3)], part_send)
-    for m in range(2):
+    for m in range(2):
+        wait_sent(stage.at[m, pl.ds(0, 12)], part_send.at[m])
         wait_sent(buf.at[m, pl.ds(0, 8)], side_send.at[m])
         wait_sent(buf.at[m, pl.ds(0, 6)], major_send.at[m])
         wait_sent(buf.at[m, 0], minor_send.at[m])
         wait_sent(buf.at[m, 0, pl.ds(0, 3)], extra_send.at[m])
-
-        def settle(ref):
-            copy = pltpu.make_async_remote_copy(
-                src_ref=ref, dst_ref=ref, send_sem=sum_send.at[m], recv_sem=sum_recv.at[m],
+        for xx in range(RING):
+            inside = (y == r) & (x == xx)
+
+            @pl.when(inside)
+            def _():
+                wait_sent(total.at[m, xx, pl.ds(0, PIECE - PAD)], sum_send.at[m, xx])
+
+            @pl.when(jnp.logical_not(inside))
+            def _():
+                wait_sent(total.at[m, xx], sum_send.at[m, xx])
+
+        def landed(ref):
+            pltpu.make_async_remote_copy(
+                src_ref=ref, dst_ref=ref, send_sem=sum_send.at[m, 0], recv_sem=sum_recv.at[m],
                 device_id=(sibling, r), device_id_type=MESH,
-            )
-            copy.wait_send()
-            copy.wait_recv()
-
-        @pl.when(alone)
+            ).wait_recv()
+
+        @pl.when(y == r)
         def _():
-            settle(final.at[m, pl.ds(0, 15)])
-
-        @pl.when(jnp.logical_not(alone))
+            landed(final.at[m, pl.ds(0, 15)])
+
+        @pl.when(y != r)
         def _():
-            settle(final.at[m])
+            landed(final.at[m])
         for k in range(16):
             out_ref[:, m, k * Q:(k + 1) * Q] = decode(final[m, k])[:ROWS, :Q]
 
@@ -349,9 +361,9 @@
             pltpu.VMEM((PAD, MAIN), jnp.float32),
             pltpu.VMEM((PIECE, TAIL), jnp.float32),
             pltpu.VMEM((PIECE, LANES), jnp.float32),
-            pltpu.VMEM((4, 32, PAD, LANES), jnp.int16),
-            pltpu.VMEM((4, 32, PAD, LANES), jnp.int16),
-            pltpu.VMEM((32, PAD, LANES), jnp.int16),
+            pltpu.VMEM((2, 16, PIECE, LANES), jnp.int16),
+            pltpu.VMEM((2, 4, 4, PIECE, LANES), jnp.int16),
+            pltpu.VMEM((2, 4, PIECE, LANES), jnp.int16),
             pltpu.VMEM((2, 16, PAD, LANES), jnp.int16),
             pltpu.SMEM((16,), jnp.int32),
             pltpu.SMEM((16,), jnp.int32),
@@ -363,9 +375,9 @@
             dma((2,)),
             dma((2,)),
             dma((2,)),
-            dma,
-            dma((16,)),
-            dma((2,)),
+            dma((2,)),
+            dma((2, 4)),
+            dma((2, 4)),
             dma((2,)),
             pltpu.SemaphoreType.REGULAR,
             pltpu.SemaphoreType.REGULAR,

time: 79.5 us -> 76.7 us (0.965)
  Pallas kernels: 77.6 us -> 74.6 us
    pallas_call x1, Pallas kernels: 77.6 us -> 74.6 us  [per_device(): pl.pallas_call(kernel, out_shape=jax.ShapeDtypeStruct((ROWS, 2, K), jnp.f...]
where the time goes in v4:
time: 76.7 us; the launch traced here: 76.3 us
  Pallas kernels  74.6 us (97%)
  local copies, waits for them, and re-layouts  1.74 us (2%)
    pallas_call x1, Pallas kernels, per_device(): pl.pallas_call(kernel, out_shape=jax.ShapeDtypeStruct((ROWS, 2, K), jnp.f...  74.6 us
    unnamed x1, local copies, waits for them, and re-layouts  1.74 us

profile of v4, /device:TPU:16, one launch (start us, length us, event | category | flops | bytes accessed | tf_op | source)
XLA Modules:
  0.0 76.3 jit_solution(12643522184354379473)
XLA Ops:
  0.0 74.6 %shard_map.46 = f32[13,2,3328]{2,1,0:T(2,128)} custom-call(s32[2]{0:T(128)} %slab_ref.1, s32[8]{0:T(128)} %virt_ref.1, bf16[13,2,3328]{2,1,0:T(2,128)(2,1)} %bitcast.3, bf16[8,208,3328]{2,1,0:T(8,128)(2,1)} %w_hbm.1), custom_call_target="tpu_custom_call" | custom-call | flops 4600000000 | bytes 12000000 | tf_op jit(solution)/shard_map/pallas_call | solution.py:353
  74.6 1.7 %copy.6 = f32[2,13,3328]{2,0,1:T(2,128)} copy(f32[2,13,3328]{2,0,1:T(2,128)} %bitcast.2) | data formatting | bytes 692224
